TPU v7x, 32 devices: a whole 2x2x4 slice. The times are simulated.
32 devices in a mesh: groups: 2 (over y), serve: 4 (over x, core), tensor: 4 (over z).
Axes of the slice: x: 2, y: 2, z: 4, core: 2. Of those that a mesh axis runs over, the one named last changes fastest.
Arguments:
- tokens: bfloat16 [4096, 8192], P(('groups', 'serve'), 'tensor'), parts along dimension 0, may hold values from -6 to 6
- base_weight: bfloat16 [8192, 4096], P('tensor'), may hold values from -0.09375 to 0.09375
- adapter_down: bfloat16 [8, 64, 8192], P('serve', None, 'tensor'), may hold values from -0.0625 to 0.0625
- adapter_up: bfloat16 [8, 64, 4096], P('serve', None, 'tensor'), may hold values from -0.75 to 0.75
- segment_adapter: int32 [16], P('groups'), parts along dimension 0, may hold values from 0 to 7
- owner_map: int32 [16], P('groups'), parts along dimension 0, may hold values from 0 to 7, as said below
- segment_blocks: int32 [16], P(('groups', 'serve')), parts along dimension 0, may hold values from 1 to 2
Outputs:
- mixed: bfloat16 [4096, 4096], P(('groups', 'serve'), 'tensor'), parts along dimension 0
There are 2 independent parts, one for each index of `groups`. A program takes and returns all parts, laid end to end along the dimension named above; an argument that names none is the same for every part. Nothing has to cross between parts.
Inputs may be any that keep to these rules, and one draw needn't show every extreme that they name: owner_map is a permutation of the store rows; the adapters named by the segments of one serve device lie in store rows of pairwise different serve devices (row // 2).
All inputs are finite; a program needn't handle non-finite values.
Results may differ from a plain program's by a relative error of at most 0.012.
Values may be sent and summed in bfloat16 or wider, within the bound.
A program may use at most 128 MiB of HBM per device.

v0:
```python
import jax
import jax.numpy as jnp
from jax import lax
from jax.sharding import PartitionSpec as P

BLOCK = 128


low_rank_scale = 0.5


def on_device(
    tokens, base_weight, adapter_down, adapter_up, segment_adapter, owner_map, segment_blocks
):
    own_index = lax.axis_index("serve")
    segment_count = segment_blocks.shape[0]
    feature_width = tokens.shape[1]
    lookup = segment_adapter[:, None] == jnp.arange(owner_map.shape[0], dtype=jnp.int32)[None, :]
    store_rows = jnp.sum(jnp.where(lookup, owner_map[None, :], 0), axis=1)
    my_rows = lax.dynamic_slice_in_dim(store_rows, own_index * segment_count, segment_count)
    pieces = (
        lax.all_gather(adapter_down, "serve", axis=0, tiled=True),
        lax.all_gather(adapter_up, "serve", axis=0, tiled=True),
    )
    row_count = pieces[0].shape[0]
    selector = (my_rows[:, None] == jnp.arange(row_count, dtype=jnp.int32)[None, :]).astype(
        jnp.bfloat16
    )
    down_part = jnp.einsum("cn,nrd->crd", selector, pieces[0], preferred_element_type=jnp.float32)
    up_part = jnp.einsum("cn,nro->cro", selector, pieces[1], preferred_element_type=jnp.float32)
    segment_down = down_part.astype(jnp.bfloat16)
    segment_expand = up_part.astype(jnp.bfloat16)
    token_segments = tokens.reshape(segment_count, -1, feature_width)
    partial_value = jnp.einsum(
        "ctd,crd->crt", token_segments, segment_down, preferred_element_type=jnp.float32
    )
    rank_reduce = lax.psum(partial_value.astype(jnp.bfloat16), "tensor")
    low_rank_delta = jnp.einsum(
        "hag,has->hgs", rank_reduce, segment_expand, preferred_element_type=jnp.float32
    )
    out_width = base_weight.shape[1] // lax.axis_size("tensor")
    base_cols = lax.psum_scatter(
        lax.dot_general(
            base_weight, tokens, (((0,), (1,)), ((), ())), preferred_element_type=jnp.float32
        ).astype(jnp.bfloat16),
        "tensor",
        scatter_dimension=0,
        tiled=True,
    ).astype(jnp.float32)
    frozen_rows = base_cols.T.reshape(segment_count, -1, out_width)
    active_rows = (
        jnp.arange(frozen_rows.shape[1], dtype=jnp.int32)[None, :] < segment_blocks[:, None] * BLOCK
    )
    mixed = jnp.where(active_rows[:, :, None], frozen_rows + low_rank_scale * low_rank_delta, 0.0)
    return mixed.reshape(-1, out_width).astype(jnp.bfloat16)


def solution(mesh):
    in_specs = (
        P(("groups", "serve"), "tensor"),
        P("tensor", None),
        P("serve", None, "tensor"),
        P("serve", None, "tensor"),
        P("groups"),
        P("groups"),
        P(("groups", "serve")),
    )
    out_specs = P(("groups", "serve"), "tensor")
    return jax.shard_map(
        on_device, mesh=mesh, in_specs=in_specs, out_specs=out_specs, check_vma=False
    )
```

profile of v0, /device:TPU:18, one launch (start us, length us, event | category | flops | bytes accessed | tf_op | source)
XLA Modules:
  0.0 147.5 jit_solution(5793370381049665000)
XLA Ops:
  7.4 0.0 copy-start
  7.4 0.0 all-gather.5.cloned.1.call-start
  7.4 0.7 all-gather.5.cloned.1.call-update
  8.1 0.0 all-gather.3.cloned.1.call-start
  8.1 0.7 all-gather.3.cloned.1.call-update
  8.8 0.0 reduce-scatter.2.cloned.1.call-start
  8.9 0.1 copy-done
  9.0 13.9 %convolution_convert_fusion = bf16[4096,512]{1,0:T(8,128)(2,1)} fusion(bf16[2048,4096]{1,0:T(8,128)(2,1)} %param.8, bf16[512,2048]{1,0:T(8,128)(2,1)S(1)} %copy-done), kind=kOutput, calls=%fused_computation | convolution fusion | flops 8592031744 | bytes 23068672 | tf_op jit(solution)/shard_map/dot_general | solution.py:43
  22.8 0.0 copy-start.1
  22.8 0.0 copy-start.2
  22.9 0.0 copy-start.3
  22.9 0.0 reduce-scatter.2.cloned.1.call-update
  22.9 0.0 all-reduce.2.cloned.1.call-start
  22.9 0.6 copy-done.1
  23.5 0.0 copy-done.2
  23.5 0.2 select_reduce_fusion
  23.7 0.1 dynamic_slice.3
  23.8 0.0 copy-done.3
  23.8 0.1 iota_compare_fusion.1
  23.9 2.9 %all-gather.5.cloned.1.call-done = bf16[8,64,1024]{2,1,0:T(8,128)(2,1)} async-done(((bf16[2,64,1024]{2,1,0:T(8,128)(2,1)}), bf16[8,64,1024]{2,1,0:T(8,128)(2,1)}) %all-gather.5.cloned.1.call-update) | async-done | bytes 1048592 | tf_op jit(solution)/shard_map/all_gather | solution.py:23
  26.7 2.0 %convolution_convert_fusion.2 = bf16[2,64,1024]{2,0,1:T(2,128)(2,1)S(1)} fusion(bf16[8,64,1024]{2,1,0:T(8,128)(2,1)} %all-gather.5.cloned.1.call-done, s32[2]{0:T(128)S(1)} %dynamic_slice.3), kind=kOutput, calls=%fused_computation.5 | convolution fusion | flops 2228240 | bytes 1310728 | tf_op jit(solution)/shard_map/cn,nro->cro/dot_general | solution.py:30
  28.7 22.3 %all-gather.3.cloned.1.call-done = bf16[8,64,2048]{2,1,0:T(8,128)(2,1)} async-done(((bf16[2,64,2048]{2,1,0:T(8,128)(2,1)}), bf16[8,64,2048]{2,1,0:T(8,128)(2,1)}) %all-gather.3.cloned.1.call-update) | async-done | bytes 2097168 | tf_op jit(solution)/shard_map/all_gather | solution.py:22
  51.0 3.1 %convolution_convert_fusion.1 = bf16[2,64,2048]{2,0,1:T(2,128)(2,1)S(1)} fusion(bf16[8,64,2048]{2,1,0:T(8,128)(2,1)} %all-gather.3.cloned.1.call-done, s32[2]{0:T(128)S(1)} %dynamic_slice.3), kind=kOutput, calls=%fused_computation.1 | convolution fusion | flops 4456464 | bytes 2621448 | tf_op jit(solution)/shard_map/cn,nrd->crd/dot_general | solution.py:29
  54.1 1.4 convolution_convert_fusion.3
  55.5 0.0 all-reduce.2.cloned.1.call-update
  55.5 45.7 %reduce-scatter.2.cloned.1.call-done = bf16[1024,512]{1,0:T(8,128)(2,1)} async-done(((bf16[4096,512]{1,0:T(8,128)(2,1)}), bf16[1024,512]{1,0:T(8,128)(2,1)}) %reduce-scatter.2.cloned.1.call-update) | async-done | bytes 1048592 | tf_op jit(solution)/shard_map/reduce_scatter | solution.py:42
  101.2 2.9 %convert_bitcast_fusion = f32[512,1024]{0,1:T(8,128)} fusion(bf16[1024,512]{1,0:T(8,128)(2,1)} %reduce-scatter.2.cloned.1.call-done), kind=kLoop, calls=%fused_computation.3 | loop fusion | flops 524288 | bytes 3145728 | tf_op jit(solution)/shard_map/reshape | solution.py:50
  104.1 2.9 %copy.15 = f32[512,1024]{1,0:T(8,128)} copy(f32[512,1024]{0,1:T(8,128)} %convert_bitcast_fusion) | data formatting | bytes 4194304 | tf_op jit(solution)/shard_map/reshape | solution.py:50
  107.0 30.0 %all-reduce.2.cloned.1.call-done = bf16[2,64,256]{2,1,0:T(8,128)(2,1)} async-done(((bf16[2,64,256]{2,1,0:T(8,128)(2,1)}), bf16[2,64,256]{2,1,0:T(8,128)(2,1)}) %all-reduce.2.cloned.1.call-update) | async-done | bytes 65552 | tf_op jit(solution)/shard_map/psum | solution.py:37
  137.0 3.1 %select_convert_fusion = bf16[2,256,1024]{2,1,0:T(8,128)(2,1)} fusion(f32[2,256,1024]{2,1,0:T(8,128)} %bitcast.15, bf16[2,64,256]{2,1,0:T(8,128)(2,1)} %all-reduce.2.cloned.1.call-done, pred[2,256]{1,0:T(4,128)(4,1)S(1)} %iota_compare_fusion.1, bf16[2,64,1024]{2,0,1:T(2,128)(2,1)S(1)} %convolution_convert_fusion.2), kind=kOutput, calls=%fused_computation.4 | convolution fusion | flops 69206016 | bytes 3473920 | tf_op jit(solution)/shard_map/hag,has->hgs/dot_general | solution.py:38
  (1 shorter events, 0.0 us)
Async XLA Ops:
  7.4 1.6 %copy-start = (bf16[512,2048]{1,0:T(8,128)(2,1)S(1)}, bf16[512,2048]{1,0:T(8,128)(2,1)}, u32[]{:S(2)}) copy-start(bf16[512,2048]{1,0:T(8,128)(2,1)} %param.7) | copy-start | bytes 6291460
  7.4 19.3 %all-gather.5.cloned.1.call-start = ((), (), s32[]{:S(2)}) async-start(), calls=%async_computation.4 | async-start | bytes 1310720 | tf_op jit(solution)/shard_map/all_gather | solution.py:23
  8.1 42.9 %all-gather.3.cloned.1.call-start = ((), (), s32[]{:S(2)}) async-start(), calls=%async_computation.2 | async-start | bytes 2621440 | tf_op jit(solution)/shard_map/all_gather | solution.py:22
  8.8 92.4 %reduce-scatter.2.cloned.1.call-start = ((), (), s32[]{:S(2)}) async-start(), calls=%async_computation.1 | async-start | bytes 5242880 | tf_op jit(solution)/shard_map/reduce_scatter | solution.py:42
  22.8 0.7 copy-start.1
  22.8 0.7 copy-start.2
  22.9 0.9 copy-start.3
  22.9 114.1 %all-reduce.2.cloned.1.call-start = ((), (), s32[]{:S(2)}) async-start(), calls=%async_computation.3 | async-start | bytes 131072 | tf_op jit(solution)/shard_map/psum | solution.py:37
Sparse Core Ops, SparseCore 0:
  9.8 16.8 all-gather.4
  28.4 22.5 all-gather.2
Sparse Core Ops, SparseCore 1:
  23.0 78.2 reduce-scatter.1
  103.5 33.4 all-reduce.1
where the time goes:
time: 150 us; the launch traced here: 148 us
  waiting for transfers between devices  102 us (68%)
  matrix products  23.5 us (16%)
  between operations  14.9 us (10%)
  local copies, waits for them, and re-layouts  3.63 us (2%)
  other arithmetic  3.12 us (2%)
    reduce_scatter x1, waiting for transfers between devices, on_device(): lax.psum_scatter(lax.dot_general(base_weight, tokens, (((0,), (1,)), ((),...  45.7 us
    psum x1, waiting for transfers between devices, on_device(): rank_reduce = lax.psum(partial_value.astype(jnp.bfloat16), 'tensor')  30 us
    all_gather x1, waiting for transfers between devices, on_device(): lax.all_gather(adapter_down, 'serve', axis=0, tiled=True)  22.3 us
    dot_general x1, matrix products, on_device(): lax.dot_general(base_weight, tokens, (((0,), (1,)), ((), ())), preferred_...  13.9 us
    dot_general x1, matrix products, on_device(): jnp.einsum('cn,nrd->crd', selector, pieces[0], preferred_element_type=jnp...  3.13 us
    dot_general x1, matrix products, on_device(): jnp.einsum('hag,has->hgs', rank_reduce, segment_expand, preferred_element...  3.09 us
  transfers between devices with their start and end apart: 4, of which 4 were waited for; matrix products, arithmetic and copies ran while one was open for 18% of the time, Pallas kernels for 0%

commit v1 on v0

v1 whole, which is shorter than its diff:
```python
import functools

import jax
import jax.numpy as jnp
from jax import lax
from jax.experimental import pallas as pl
from jax.experimental.pallas import tpu as pltpu
from jax.sharding import PartitionSpec as P

MESH = pl.DeviceIdType.MESH
BLOCK = 128
WIDTH = 256
AHEAD = 3

low_rank_scale = 0.5


def kernel(
    n,
    n_serve,
    seg_adapter,
    owner_map,
    tok_hbm,
    w_hbm,
    down_hbm,
    up_hbm,
    out_hbm,
    tok,
    w,
    acc,
    send,
    from_left,
    from_right,
    own,
    out,
    down,
    up,
    down_send,
    up_send,
    down_got,
    up_got,
    rank_own,
    rank_send,
    rank_got,
    local_sem,
    w_sem,
    out_sem,
    send_sem,
    left_sem,
    right_sem,
    down_ssem,
    down_rsem,
    up_ssem,
    up_rsem,
    rank_ssem,
    rank_rsem,
):
    z = lax.axis_index("tensor")
    me = lax.axis_index("serve")
    chunks = w.shape[0]
    per = chunks // n
    steps = chunks - per
    stored, rank = down.shape[0], down.shape[1]
    rows = tok.shape[0]
    segs = seg_adapter.shape[0] // n_serve
    seg_len = rows // segs
    first_right = (z + 1) * per
    first_own = z * per

    def load_w(q):
        return pltpu.make_async_copy(
            w_hbm.at[:, pl.ds(pl.multiple_of(q * WIDTH, WIDTH), WIDTH)], w.at[q], w_sem.at[q]
        )

    load_tok = pltpu.make_async_copy(tok_hbm, tok, local_sem.at[0])
    load_down = pltpu.make_async_copy(down_hbm, down, local_sem.at[1])
    load_up = pltpu.make_async_copy(up_hbm, up, local_sem.at[2])

    barrier = pltpu.get_barrier_semaphore()

    @pl.loop(1, n_serve)
    def _(k):
        pl.semaphore_signal(
            barrier, inc=1, device_id={"serve": lax.rem(me + k, n_serve)}, device_id_type=MESH
        )

    @pl.when(z > 0)
    def _():
        pl.semaphore_signal(barrier, inc=1, device_id={"tensor": z - 1}, device_id_type=MESH)

    @pl.when(z < n - 1)
    def _():
        pl.semaphore_signal(barrier, inc=1, device_id={"tensor": z + 1}, device_id_type=MESH)

    load_tok.start()

    def load_step(i):
        @pl.when(chunks - 1 - i >= first_right)
        def _():
            load_w(chunks - 1 - i).start()

        @pl.when(i < first_own)
        def _():
            load_w(i).start()

    load_step(0)
    load_down.start()
    load_up.start()

    @pl.loop(1, steps)
    def _(i):
        load_step(i)

    @pl.loop(0, per)
    def _(c):
        load_w(first_own + c).start()

    def row_for(peer):
        row = jnp.int32(0)
        for j in range(segs):
            stored_row = owner_map[seg_adapter[peer * segs + j]]
            row += jnp.where(lax.div(stored_row, stored) == me, lax.rem(stored_row, stored), 0)
        return row

    def owner_of(j):
        return lax.div(owner_map[seg_adapter[me * segs + j]], stored)

    def adapter_copy(k, src, dst, ssem, rsem):
        peer = lax.rem(me + k, n_serve)
        return pltpu.make_async_remote_copy(
            src_ref=src.at[peer],
            dst_ref=dst.at[me],
            send_sem=ssem.at[peer],
            recv_sem=rsem.at[me],
            device_id={"serve": peer},
            device_id_type=MESH,
        )

    def adapter_wait(k, src, dst, ssem, rsem):
        peer = lax.rem(me + k, n_serve)
        got = pltpu.make_async_remote_copy(
            src_ref=src.at[peer],
            dst_ref=dst.at[peer],
            send_sem=ssem.at[peer],
            recv_sem=rsem.at[peer],
            device_id={"serve": peer},
            device_id_type=MESH,
        )
        got.wait_send()
        got.wait_recv()

    load_down.wait()
    neighbours = (z > 0).astype(jnp.int32) + (z < n - 1).astype(jnp.int32)
    pl.semaphore_wait(barrier, n_serve - 1 + neighbours)

    @pl.loop(1, n_serve)
    def _(k):
        peer = lax.rem(me + k, n_serve)
        down_send[peer] = down[row_for(peer)]
        adapter_copy(k, down_send, down_got, down_ssem, down_rsem).start()

    down_got[me] = down[row_for(me)]
    load_tok.wait()

    def chunk_copy(q, to_right):
        return pltpu.make_async_remote_copy(
            src_ref=send.at[q],
            dst_ref=(from_left if to_right else from_right).at[q],
            send_sem=send_sem.at[q],
            recv_sem=(left_sem if to_right else right_sem).at[q],
            device_id={"tensor": z + 1 if to_right else z - 1},
            device_id_type=MESH,
        )

    def rank_copy(to_right):
        side = 0 if to_right else 1
        return pltpu.make_async_remote_copy(
            src_ref=rank_send.at[side],
            dst_ref=rank_got.at[side],
            send_sem=rank_ssem.at[side],
            recv_sem=rank_rsem.at[side],
            device_id={"tensor": z + 1 if to_right else z - 1},
            device_id_type=MESH,
        )

    def base_step(i, q, to_right):
        load_w(q).wait()
        acc[...] = jnp.dot(tok[...], w[q], preferred_element_type=jnp.float32)
        behind = (z > 0) if to_right else (z < n - 1)

        @pl.when(behind)
        def _():
            chunk_copy(q, to_right).wait_recv()
            got = (from_left if to_right else from_right)[q]
            send[q] = (acc[...] + got.astype(jnp.float32)).astype(jnp.bfloat16)

        @pl.when(jnp.logical_not(behind))
        def _():
            send[q] = acc[...].astype(jnp.bfloat16)

        @pl.when(i >= AHEAD)
        def _():
            chunk_copy(q + AHEAD if to_right else q - AHEAD, to_right).wait_send()

        chunk_copy(q, to_right).start()

    def base_steps(i):
        @pl.when(chunks - 1 - i >= first_right)
        def _():
            base_step(i, chunks - 1 - i, True)

        @pl.when(i < first_own)
        def _():
            base_step(i, i, False)

    def rank_steps():
        @pl.loop(1, n_serve)
        def _(k):
            adapter_wait(k, down_send, down_got, down_ssem, down_rsem)

        for j in range(segs):
            at = pl.ds(j * seg_len, seg_len)
            rank_own[:, at] = lax.dot_general(
                down_got[owner_of(j)],
                tok[at, :],
                (((1,), (1,)), ((), ())),
                preferred_element_type=jnp.float32,
            )
        for to_right in (True, False):
            side = 0 if to_right else 1
            behind = (z > 0) if to_right else (z < n - 1)
            ahead = (z < n - 1) if to_right else (z > 0)

            @pl.when(behind)
            def _():
                rank_copy(to_right).wait_recv()

                @pl.when(ahead)
                def _():
                    rank_send[side] = (
                        rank_own[...] + rank_got[side].astype(jnp.float32)
                    ).astype(jnp.bfloat16)

            @pl.when(jnp.logical_not(behind))
            def _():
                rank_got[side] = jnp.zeros(rank_got.shape[1:], rank_got.dtype)

                @pl.when(ahead)
                def _():
                    rank_send[side] = rank_own[...].astype(jnp.bfloat16)

            @pl.when(ahead)
            def _():
                rank_copy(to_right).start()

    middle = min(6, steps - 1)

    @pl.loop(0, 2)
    def _(i):
        base_steps(i)

    load_up.wait()

    @pl.loop(1, n_serve)
    def _(k):
        peer = lax.rem(me + k, n_serve)
        up_send[peer] = up[row_for(peer)]
        adapter_copy(k, up_send, up_got, up_ssem, up_rsem).start()

    up_got[me] = up[row_for(me)]

    @pl.loop(2, steps)
    def _(i):
        base_steps(i)

        @pl.when(i == middle)
        def _():
            rank_steps()

    @pl.loop(1, n_serve)
    def _(k):
        adapter_wait(k, up_send, up_got, up_ssem, up_rsem)

    coords = (
        rank_own[...] + rank_got[0].astype(jnp.float32) + rank_got[1].astype(jnp.float32)
    ).astype(jnp.bfloat16)
    for c in range(per):
        load_w(first_own + c).wait()
        own[c] = jnp.dot(tok[...], w[first_own + c], preferred_element_type=jnp.float32)
        for j in range(segs):
            at = pl.ds(j * seg_len, seg_len)
            own[c, at, :] += low_rank_scale * lax.dot_general(
                coords[:, j * seg_len : (j + 1) * seg_len],
                up_got[owner_of(j), :, c * WIDTH : (c + 1) * WIDTH],
                (((0,), (0,)), ((), ())),
                preferred_element_type=jnp.float32,
            )

    def out_copy(c):
        return pltpu.make_async_copy(
            out.at[c], out_hbm.at[:, pl.ds(pl.multiple_of(c * WIDTH, WIDTH), WIDTH)], out_sem.at[c]
        )

    @pl.loop(0, per)
    def _(k):
        c = jnp.where(2 * z < n, per - 1 - k, k)
        q = first_own + c

        @pl.when(z > 0)
        def _():
            chunk_copy(q, True).wait_recv()
            own[c] += from_left[q].astype(jnp.float32)

        @pl.when(z < n - 1)
        def _():
            chunk_copy(q, False).wait_recv()
            own[c] += from_right[q].astype(jnp.float32)

        out[c] = own[c].astype(jnp.bfloat16)
        out_copy(c).start()

    @pl.loop(0, per)
    def _(c):
        out_copy(c).wait()

    @pl.loop(0, steps)
    def _(i):
        @pl.when((chunks - 1 - i >= first_right) & (chunks - 1 - i - AHEAD < first_right))
        def _():
            chunk_copy(chunks - 1 - i, True).wait_send()

        @pl.when((i < first_own) & (i + AHEAD >= first_own))
        def _():
            chunk_copy(i, False).wait_send()

    @pl.when(z < n - 1)
    def _():
        rank_copy(True).wait_send()

    @pl.when(z > 0)
    def _():
        rank_copy(False).wait_send()


def on_device(
    n,
    n_serve,
    tokens,
    base_weight,
    adapter_down,
    adapter_up,
    segment_adapter,
    owner_map,
    segment_blocks,
):
    rows, depth = tokens.shape
    columns = base_weight.shape[1]
    chunks = columns // WIDTH
    out_width = columns // n
    per = out_width // WIDTH
    stored, rank, _ = adapter_down.shape
    bf16, f32 = jnp.bfloat16, jnp.float32
    smem = pl.BlockSpec(memory_space=pltpu.SMEM)
    anywhere = pl.BlockSpec(memory_space=pl.ANY)
    dma = pltpu.SemaphoreType.DMA
    summed = pl.pallas_call(
        functools.partial(kernel, n, n_serve),
        out_shape=jax.ShapeDtypeStruct((rows, out_width), bf16),
        in_specs=[smem, smem, anywhere, anywhere, anywhere, anywhere],
        out_specs=anywhere,
        scratch_shapes=[
            pltpu.VMEM((rows, depth), bf16),
            pltpu.VMEM((chunks, depth, WIDTH), bf16),
            pltpu.VMEM((rows, WIDTH), f32),
            pltpu.VMEM((chunks, rows, WIDTH), bf16),
            pltpu.VMEM((chunks, rows, WIDTH), bf16),
            pltpu.VMEM((chunks, rows, WIDTH), bf16),
            pltpu.VMEM((per, rows, WIDTH), f32),
            pltpu.VMEM((per, rows, WIDTH), bf16),
            pltpu.VMEM((stored, rank, depth), bf16),
            pltpu.VMEM((stored, rank, out_width), bf16),
            pltpu.VMEM((n_serve, rank, depth), bf16),
            pltpu.VMEM((n_serve, rank, out_width), bf16),
            pltpu.VMEM((n_serve, rank, depth), bf16),
            pltpu.VMEM((n_serve, rank, out_width), bf16),
            pltpu.VMEM((rank, rows), f32),
            pltpu.VMEM((2, rank, rows), bf16),
            pltpu.VMEM((2, rank, rows), bf16),
            dma((3,)),
            dma((chunks,)),
            dma((per,)),
            dma((chunks,)),
            dma((chunks,)),
            dma((chunks,)),
            dma((n_serve,)),
            dma((n_serve,)),
            dma((n_serve,)),
            dma((n_serve,)),
            dma((2,)),
            dma((2,)),
        ],
        compiler_params=pltpu.CompilerParams(
            collective_id=0, has_side_effects=True, vmem_limit_bytes=56 * 2**20
        ),
        cost_estimate=pl.CostEstimate(
            flops=2 * rows * depth * columns,
            bytes_accessed=2 * (depth * columns + rows * depth + rows * out_width),
            transcendentals=0,
        ),
    )(segment_adapter, owner_map, tokens, base_weight, adapter_down, adapter_up)
    segments = segment_blocks.shape[0]
    live = jnp.arange(rows // segments, dtype=jnp.int32)[None, :] < segment_blocks[:, None] * BLOCK
    return jnp.where(live.reshape(-1)[:, None], summed, jnp.zeros((), bf16))


def solution(mesh):
    in_specs = (
        P(("groups", "serve"), "tensor"),
        P("tensor", None),
        P("serve", None, "tensor"),
        P("serve", None, "tensor"),
        P("groups"),
        P("groups"),
        P(("groups", "serve")),
    )
    out_specs = P(("groups", "serve"), "tensor")
    return jax.shard_map(
        functools.partial(on_device, mesh.shape["tensor"], mesh.shape["serve"]),
        mesh=mesh,
        in_specs=in_specs,
        out_specs=out_specs,
        check_vma=False,
    )
```

time: 150 us -> 113 us (0.75)
  the two profiles are of different devices: /device:TPU:18 before, /device:TPU:8 now
where the time goes in v1:
time: 113 us
  Pallas kernels  110 us (97%)
  other arithmetic  3.07 us (3%)
    pallas_call x1, Pallas kernels, on_device(): pl.pallas_call(functools.partial(kernel, n, n_serve), out_shape=jax.Shape...  110 us
    select_n x1, other arithmetic, on_device(): return jnp.where(live.reshape(-1)[:, None], summed, jnp.zeros((), bf16))  2.34 us

profile of v1, /device:TPU:8, one launch (start us, length us, event | category | flops | bytes accessed | tf_op | source)
XLA Modules:
  0.0 112.7 jit_solution(527956416547490232)
XLA Ops:
  0.0 0.7 broadcast_multiply_fusion
  0.7 0.1 iota_compare_fusion
  0.8 109.6 %shard_map.73 = bf16[512,1024]{1,0:T(8,128)(2,1)} custom-call(s32[8]{0:T(128)} %seg_adapter.1, s32[8]{0:T(128)} %owner_map.1, bf16[512,2048]{1,0:T(8,128)(2,1)} %tok_hbm.1, bf16[2048,4096]{1,0:T(8,128)(2,1)} %w_hbm.1, bf16[2,64,2048]{2,1,0:T(8,128)(2,1)} %down_hbm.1, bf16[2,64,1024]{2,1,0:T(8,128)(2,1)} %up_hbm.1), custom_call_target="tpu_custom_call" | custom-call | flops 8589934592 | bytes 19922944 | tf_op jit(solution)/shard_map/pallas_call | solution.py:366
  110.4 2.3 %broadcast_select_fusion = bf16[512,1024]{1,0:T(8,128)(2,1)} fusion(bf16[512,1024]{1,0:T(8,128)(2,1)} %shard_map.73, pred[512]{0:T(512)(128)(4,1)S(1)} %lt.23), kind=kLoop, calls=%fused_computation | loop fusion | flops 524288 | bytes 2097664 | tf_op jit(solution)/shard_map/jit(_where)/select_n | solution.py:413
  (1 shorter events, 0.0 us)

commit v2 on v1

--- a/solution.py
+++ b/solution.py
@@ -10,6 +10,8 @@
 MESH = pl.DeviceIdType.MESH
 BLOCK = 128
 WIDTH = 256
+RANK_STEP = 3
+RANK_LAG = 4
 AHEAD = 3
 
 low_rank_scale = 0.5
@@ -204,16 +206,19 @@
 
         chunk_copy(q, to_right).start()
 
-    def base_steps(i):
-        @pl.when(chunks - 1 - i >= first_right)
-        def _():
-            base_step(i, chunks - 1 - i, True)
-
-        @pl.when(i < first_own)
-        def _():
-            base_step(i, i, False)
-
-    def rank_steps():
+    def base_steps(step):
+        right = step - z
+        left = step - (n - 1 - z)
+
+        @pl.when((right >= 0) & (chunks - 1 - right >= first_right))
+        def _():
+            base_step(right, chunks - 1 - right, True)
+
+        @pl.when((left >= 0) & (left < first_own))
+        def _():
+            base_step(left, left, False)
+
+    def rank_partial():
         @pl.loop(1, n_serve)
         def _(k):
             adapter_wait(k, down_send, down_got, down_ssem, down_rsem)
@@ -226,34 +231,39 @@
                 (((1,), (1,)), ((), ())),
                 preferred_element_type=jnp.float32,
             )
-        for to_right in (True, False):
-            side = 0 if to_right else 1
-            behind = (z > 0) if to_right else (z < n - 1)
-            ahead = (z < n - 1) if to_right else (z > 0)
-
-            @pl.when(behind)
-            def _():
-                rank_copy(to_right).wait_recv()
-
-                @pl.when(ahead)
-                def _():
-                    rank_send[side] = (
-                        rank_own[...] + rank_got[side].astype(jnp.float32)
-                    ).astype(jnp.bfloat16)
-
-            @pl.when(jnp.logical_not(behind))
-            def _():
-                rank_got[side] = jnp.zeros(rank_got.shape[1:], rank_got.dtype)
-
-                @pl.when(ahead)
-                def _():
-                    rank_send[side] = rank_own[...].astype(jnp.bfloat16)
+
+    def rank_hop(to_right):
+        side = 0 if to_right else 1
+        behind = (z > 0) if to_right else (z < n - 1)
+        ahead = (z < n - 1) if to_right else (z > 0)
+
+        @pl.when(behind)
+        def _():
+            rank_copy(to_right).wait_recv()
 
             @pl.when(ahead)
             def _():
-                rank_copy(to_right).start()
-
-    middle = min(6, steps - 1)
+                rank_send[side] = (
+                    rank_own[...] + rank_got[side].astype(jnp.float32)
+                ).astype(jnp.bfloat16)
+
+        @pl.when(jnp.logical_not(behind))
+        def _():
+            rank_got[side] = jnp.zeros(rank_got.shape[1:], rank_got.dtype)
+
+            @pl.when(ahead)
+            def _():
+                rank_send[side] = rank_own[...].astype(jnp.bfloat16)
+
+        @pl.when(ahead)
+        def _():
+            rank_copy(to_right).start()
+
+    last = steps + n - 2
+    first_rank = min(RANK_STEP, last)
+
+    def rank_step_of(distance):
+        return jnp.minimum(first_rank + RANK_LAG * distance, last)
 
     @pl.loop(0, 2)
     def _(i):
@@ -269,13 +279,21 @@
 
     up_got[me] = up[row_for(me)]
 
-    @pl.loop(2, steps)
+    @pl.loop(2, last + 1)
     def _(i):
         base_steps(i)
 
-        @pl.when(i == middle)
-        def _():
-            rank_steps()
+        @pl.when(i == first_rank)
+        def _():
+            rank_partial()
+
+        @pl.when(i == rank_step_of(z))
+        def _():
+            rank_hop(True)
+
+        @pl.when(i == rank_step_of(n - 1 - z))
+        def _():
+            rank_hop(False)
 
     @pl.loop(1, n_serve)
     def _(k):

time: 113 us -> 79.5 us (0.70)
  the two profiles are of different devices: /device:TPU:8 before, /device:TPU:18 now
where the time goes in v2:
time: 79.5 us; the launch traced here: 79.3 us
  Pallas kernels  76.2 us (96%)
  other arithmetic  3.07 us (4%)
    pallas_call x1, Pallas kernels, on_device(): pl.pallas_call(functools.partial(kernel, n, n_serve), out_shape=jax.Shape...  76.2 us
    select_n x1, other arithmetic, on_device(): return jnp.where(live.reshape(-1)[:, None], summed, jnp.zeros((), bf16))  2.34 us

profile of v2, /device:TPU:18, one launch (start us, length us, event | category | flops | bytes accessed | tf_op | source)
XLA Modules:
  0.0 79.3 jit_solution(5477549973599871097)
XLA Ops:
  0.0 0.7 broadcast_multiply_fusion
  0.7 0.1 iota_compare_fusion
  0.8 76.2 %shard_map.73 = bf16[512,1024]{1,0:T(8,128)(2,1)} custom-call(s32[8]{0:T(128)} %seg_adapter.1, s32[8]{0:T(128)} %owner_map.1, bf16[512,2048]{1,0:T(8,128)(2,1)} %tok_hbm.1, bf16[2048,4096]{1,0:T(8,128)(2,1)} %w_hbm.1, bf16[2,64,2048]{2,1,0:T(8,128)(2,1)} %down_hbm.1, bf16[2,64,1024]{2,1,0:T(8,128)(2,1)} %up_hbm.1), custom_call_target="tpu_custom_call" | custom-call | flops 8589934592 | bytes 19922944 | tf_op jit(solution)/shard_map/pallas_call | solution.py:384
  77.0 2.3 %broadcast_select_fusion = bf16[512,1024]{1,0:T(8,128)(2,1)} fusion(bf16[512,1024]{1,0:T(8,128)(2,1)} %shard_map.73, pred[512]{0:T(512)(128)(4,1)S(1)} %lt.23), kind=kLoop, calls=%fused_computation | loop fusion | flops 524288 | bytes 2097664 | tf_op jit(solution)/shard_map/jit(_where)/select_n | solution.py:431
  (1 shorter events, 0.0 us)

commit v3 on v2

--- a/solution.py
+++ b/solution.py
@@ -22,11 +22,12 @@
     n_serve,
     seg_adapter,
     owner_map,
+    seg_blocks,
     tok_hbm,
     w_hbm,
     down_hbm,
     up_hbm,
-    out_hbm,
+    out,
     tok,
     w,
     acc,
@@ -34,7 +35,6 @@
     from_left,
     from_right,
     own,
-    out,
     down,
     up,
     down_send,
@@ -46,7 +46,6 @@
     rank_got,
     local_sem,
     w_sem,
-    out_sem,
     send_sem,
     left_sem,
     right_sem,
@@ -151,18 +150,22 @@
         got.wait_send()
         got.wait_recv()
 
-    load_down.wait()
+    def product(q):
+        load_w(q).wait()
+        return jnp.dot(tok[...], w[q], preferred_element_type=jnp.float32)
+
+    load_tok.wait()
+
+    @pl.when(z == 0)
+    def _():
+        send[chunks - 1] = product(chunks - 1).astype(jnp.bfloat16)
+
+    @pl.when(z == n - 1)
+    def _():
+        send[0] = product(0).astype(jnp.bfloat16)
+
     neighbours = (z > 0).astype(jnp.int32) + (z < n - 1).astype(jnp.int32)
     pl.semaphore_wait(barrier, n_serve - 1 + neighbours)
-
-    @pl.loop(1, n_serve)
-    def _(k):
-        peer = lax.rem(me + k, n_serve)
-        down_send[peer] = down[row_for(peer)]
-        adapter_copy(k, down_send, down_got, down_ssem, down_rsem).start()
-
-    down_got[me] = down[row_for(me)]
-    load_tok.wait()
 
     def chunk_copy(q, to_right):
         return pltpu.make_async_remote_copy(
@@ -185,9 +188,25 @@
             device_id_type=MESH,
         )
 
+    @pl.when(z == 0)
+    def _():
+        chunk_copy(chunks - 1, True).start()
+
+    @pl.when(z == n - 1)
+    def _():
+        chunk_copy(0, False).start()
+
+    load_down.wait()
+
+    @pl.loop(1, n_serve)
+    def _(k):
+        peer = lax.rem(me + k, n_serve)
+        down_send[peer] = down[row_for(peer)]
+        adapter_copy(k, down_send, down_got, down_ssem, down_rsem).start()
+
+    down_got[me] = down[row_for(me)]
     def base_step(i, q, to_right):
-        load_w(q).wait()
-        acc[...] = jnp.dot(tok[...], w[q], preferred_element_type=jnp.float32)
+        acc[...] = product(q)
         behind = (z > 0) if to_right else (z < n - 1)
 
         @pl.when(behind)
@@ -265,9 +284,7 @@
     def rank_step_of(distance):
         return jnp.minimum(first_rank + RANK_LAG * distance, last)
 
-    @pl.loop(0, 2)
-    def _(i):
-        base_steps(i)
+    base_steps(1)
 
     load_up.wait()
 
@@ -303,8 +320,7 @@
         rank_own[...] + rank_got[0].astype(jnp.float32) + rank_got[1].astype(jnp.float32)
     ).astype(jnp.bfloat16)
     for c in range(per):
-        load_w(first_own + c).wait()
-        own[c] = jnp.dot(tok[...], w[first_own + c], preferred_element_type=jnp.float32)
+        own[c] = product(first_own + c)
         for j in range(segs):
             at = pl.ds(j * seg_len, seg_len)
             own[c, at, :] += low_rank_scale * lax.dot_general(
@@ -314,32 +330,46 @@
                 preferred_element_type=jnp.float32,
             )
 
-    def out_copy(c):
-        return pltpu.make_async_copy(
-            out.at[c], out_hbm.at[:, pl.ds(pl.multiple_of(c * WIDTH, WIDTH), WIDTH)], out_sem.at[c]
-        )
-
-    @pl.loop(0, per)
-    def _(k):
-        c = jnp.where(2 * z < n, per - 1 - k, k)
-        q = first_own + c
-
-        @pl.when(z > 0)
-        def _():
-            chunk_copy(q, True).wait_recv()
-            own[c] += from_left[q].astype(jnp.float32)
-
-        @pl.when(z < n - 1)
-        def _():
-            chunk_copy(q, False).wait_recv()
-            own[c] += from_right[q].astype(jnp.float32)
-
-        out[c] = own[c].astype(jnp.bfloat16)
-        out_copy(c).start()
-
-    @pl.loop(0, per)
-    def _(c):
-        out_copy(c).wait()
+    def finish(c, got):
+        for j in range(segs):
+            at = pl.ds(j * seg_len, seg_len)
+            total = own[c, at, :] + got[first_own + c, at, :].astype(jnp.float32)
+            row = lax.broadcasted_iota(jnp.int32, total.shape, 0)
+            total = jnp.where(row < seg_blocks[j] * BLOCK, total, 0.0)
+            out[at, pl.ds(pl.multiple_of(c * WIDTH, WIDTH), WIDTH)] = total.astype(jnp.bfloat16)
+
+    @pl.when(2 * z < n)
+    def _():
+        @pl.loop(0, per)
+        def _(k):
+            c = per - 1 - k
+            chunk_copy(first_own + c, False).wait_recv()
+
+            @pl.when(z > 0)
+            def _():
+                own[c] += from_right[first_own + c].astype(jnp.float32)
+                chunk_copy(first_own + c, True).wait_recv()
+                finish(c, from_left)
+
+            @pl.when(z == 0)
+            def _():
+                finish(c, from_right)
+
+    @pl.when(2 * z >= n)
+    def _():
+        @pl.loop(0, per)
+        def _(c):
+            chunk_copy(first_own + c, True).wait_recv()
+
+            @pl.when(z < n - 1)
+            def _():
+                own[c] += from_left[first_own + c].astype(jnp.float32)
+                chunk_copy(first_own + c, False).wait_recv()
+                finish(c, from_right)
+
+            @pl.when(z == n - 1)
+            def _():
+                finish(c, from_left)
 
     @pl.loop(0, steps)
     def _(i):
@@ -381,11 +411,11 @@
     smem = pl.BlockSpec(memory_space=pltpu.SMEM)
     anywhere = pl.BlockSpec(memory_space=pl.ANY)
     dma = pltpu.SemaphoreType.DMA
-    summed = pl.pallas_call(
+    return pl.pallas_call(
         functools.partial(kernel, n, n_serve),
-        out_shape=jax.ShapeDtypeStruct((rows, out_width), bf16),
-        in_specs=[smem, smem, anywhere, anywhere, anywhere, anywhere],
-        out_specs=anywhere,
+        out_shape=pltpu.VMEM((rows, out_width), bf16),
+        in_specs=[smem, smem, smem, anywhere, anywhere, anywhere, anywhere],
+        out_specs=pl.BlockSpec(memory_space=pltpu.VMEM),
         scratch_shapes=[
             pltpu.VMEM((rows, depth), bf16),
             pltpu.VMEM((chunks, depth, WIDTH), bf16),
@@ -394,7 +424,6 @@
             pltpu.VMEM((chunks, rows, WIDTH), bf16),
             pltpu.VMEM((chunks, rows, WIDTH), bf16),
             pltpu.VMEM((per, rows, WIDTH), f32),
-            pltpu.VMEM((per, rows, WIDTH), bf16),
             pltpu.VMEM((stored, rank, depth), bf16),
             pltpu.VMEM((stored, rank, out_width), bf16),
             pltpu.VMEM((n_serve, rank, depth), bf16),
@@ -406,7 +435,6 @@
             pltpu.VMEM((2, rank, rows), bf16),
             dma((3,)),
             dma((chunks,)),
-            dma((per,)),
             dma((chunks,)),
             dma((chunks,)),
             dma((chunks,)),
@@ -425,10 +453,15 @@
             bytes_accessed=2 * (depth * columns + rows * depth + rows * out_width),
             transcendentals=0,
         ),
-    )(segment_adapter, owner_map, tokens, base_weight, adapter_down, adapter_up)
-    segments = segment_blocks.shape[0]
-    live = jnp.arange(rows // segments, dtype=jnp.int32)[None, :] < segment_blocks[:, None] * BLOCK
-    return jnp.where(live.reshape(-1)[:, None], summed, jnp.zeros((), bf16))
+    )(
+        segment_adapter,
+        owner_map,
+        segment_blocks,
+        tokens,
+        base_weight,
+        adapter_down,
+        adapter_up,
+    )
 
 
 def solution(mesh):

time: 79.5 us -> 76.7 us (0.965)
  other arithmetic: 3.07 us -> 0 us
  local copies, waits for them, and re-layouts: 0.02 us -> 0.97 us
    select_n x1 -> x0, other arithmetic: 2.34 us -> none  [on_device(): return jnp.where(live.reshape(-1)[:, None], summed, jnp.zeros((), bf16))]
    unnamed x0 -> x1, local copies, waits for them, and re-layouts: none -> 0.97 us
where the time goes in v3:
time: 76.7 us; the launch traced here: 76.5 us
  Pallas kernels  75.6 us (99%)
  local copies, waits for them, and re-layouts  0.97 us (1%)
    pallas_call x1, Pallas kernels, on_device(): pl.pallas_call(functools.partial(kernel, n, n_serve), out_shape=pltpu.VME...  75.6 us

profile of v3, /device:TPU:18, one launch (start us, length us, event | category | flops | bytes accessed | tf_op | source)
XLA Modules:
  0.0 76.5 jit_solution(11926380440570901916)
XLA Ops:
  0.0 75.6 %shard_map.73 = bf16[512,1024]{1,0:T(8,128)(2,1)S(1)} custom-call(s32[8]{0:T(128)} %seg_adapter.1, s32[8]{0:T(128)} %owner_map.1, s32[2]{0:T(128)} %seg_blocks.1, bf16[512,2048]{1,0:T(8,128)(2,1)} %tok_hbm.1, bf16[2048,4096]{1,0:T(8,128)(2,1)} %w_hbm.1, bf16[2,64,2048]{2,1,0:T(8,128)(2,1)} %down_hbm.1, bf16[2,64,1024]{2,1,0:T(8,128)(2,1)} %up_hbm.1), custom_call_target="tpu_custom_call" | custom-call | flops 8589934592 | bytes 19922944 | tf_op jit(solution)/shard_map/pallas_call | solution.py:414
  75.6 1.0 %copy.9 = bf16[512,1024]{1,0:T(8,128)(2,1)} copy(bf16[512,1024]{1,0:T(8,128)(2,1)S(1)} %shard_map.73) | data formatting | bytes 2097152

commit v4 on v3

--- a/solution.py
+++ b/solution.py
@@ -73,10 +73,27 @@
             w_hbm.at[:, pl.ds(pl.multiple_of(q * WIDTH, WIDTH), WIDTH)], w.at[q], w_sem.at[q]
         )
 
-    load_tok = pltpu.make_async_copy(tok_hbm, tok, local_sem.at[0])
+    half = rows // 2
+
+    def load_tok(h):
+        at = pl.ds(h * half, half)
+        return pltpu.make_async_copy(tok_hbm.at[at, :], tok.at[at, :], local_sem.at[3 * h])
+
     load_down = pltpu.make_async_copy(down_hbm, down, local_sem.at[1])
     load_up = pltpu.make_async_copy(up_hbm, up, local_sem.at[2])
 
+    def load_step(i):
+        @pl.when(chunks - 1 - i >= first_right)
+        def _():
+            load_w(chunks - 1 - i).start()
+
+        @pl.when(i < first_own)
+        def _():
+            load_w(i).start()
+
+    load_tok(0).start()
+    load_step(0)
+    load_tok(1).start()
     barrier = pltpu.get_barrier_semaphore()
 
     @pl.loop(1, n_serve)
@@ -92,29 +109,6 @@
     @pl.when(z < n - 1)
     def _():
         pl.semaphore_signal(barrier, inc=1, device_id={"tensor": z + 1}, device_id_type=MESH)
-
-    load_tok.start()
-
-    def load_step(i):
-        @pl.when(chunks - 1 - i >= first_right)
-        def _():
-            load_w(chunks - 1 - i).start()
-
-        @pl.when(i < first_own)
-        def _():
-            load_w(i).start()
-
-    load_step(0)
-    load_down.start()
-    load_up.start()
-
-    @pl.loop(1, steps)
-    def _(i):
-        load_step(i)
-
-    @pl.loop(0, per)
-    def _(c):
-        load_w(first_own + c).start()
 
     def row_for(peer):
         row = jnp.int32(0)
@@ -154,15 +148,34 @@
         load_w(q).wait()
         return jnp.dot(tok[...], w[q], preferred_element_type=jnp.float32)
 
-    load_tok.wait()
+    def first_half(q, h):
+        at = pl.ds(h * half, half)
+        send[q, at, :] = jnp.dot(tok[at, :], w[q], preferred_element_type=jnp.float32).astype(
+            jnp.bfloat16
+        )
+
+    load_tok(0).wait()
 
     @pl.when(z == 0)
     def _():
-        send[chunks - 1] = product(chunks - 1).astype(jnp.bfloat16)
+        load_w(chunks - 1).wait()
+        first_half(chunks - 1, 0)
 
     @pl.when(z == n - 1)
     def _():
-        send[0] = product(0).astype(jnp.bfloat16)
+        load_w(0).wait()
+        first_half(0, 0)
+
+    load_down.start()
+    load_up.start()
+
+    @pl.loop(1, steps)
+    def _(i):
+        load_step(i)
+
+    @pl.loop(0, per)
+    def _(c):
+        load_w(first_own + c).start()
 
     neighbours = (z > 0).astype(jnp.int32) + (z < n - 1).astype(jnp.int32)
     pl.semaphore_wait(barrier, n_serve - 1 + neighbours)
@@ -188,13 +201,36 @@
             device_id_type=MESH,
         )
 
+    def half_copy(q, h, to_right):
+        at = pl.ds(h * half, half)
+        return pltpu.make_async_remote_copy(
+            src_ref=send.at[q, at, :],
+            dst_ref=(from_left if to_right else from_right).at[q, at, :],
+            send_sem=send_sem.at[q],
+            recv_sem=(left_sem if to_right else right_sem).at[q],
+            device_id={"tensor": z + 1 if to_right else z - 1},
+            device_id_type=MESH,
+        )
+
     @pl.when(z == 0)
     def _():
-        chunk_copy(chunks - 1, True).start()
+        half_copy(chunks - 1, 0, True).start()
 
     @pl.when(z == n - 1)
     def _():
-        chunk_copy(0, False).start()
+        half_copy(0, 0, False).start()
+
+    load_tok(1).wait()
+
+    @pl.when(z == 0)
+    def _():
+        first_half(chunks - 1, 1)
+        half_copy(chunks - 1, 1, True).start()
+
+    @pl.when(z == n - 1)
+    def _():
+        first_half(0, 1)
+        half_copy(0, 1, False).start()
 
     load_down.wait()
 
@@ -433,7 +469,7 @@
             pltpu.VMEM((rank, rows), f32),
             pltpu.VMEM((2, rank, rows), bf16),
             pltpu.VMEM((2, rank, rows), bf16),
-            dma((3,)),
+            dma((4,)),
             dma((chunks,)),
             dma((chunks,)),
             dma((chunks,)),

time: 76.7 us -> 76 us (level)
  no operation moved by 1% of the time
where the time goes in v4:
time: 76 us; the launch traced here: 75.9 us
  Pallas kernels  74.9 us (99%)
  local copies, waits for them, and re-layouts  0.97 us (1%)
    pallas_call x1, Pallas kernels, on_device(): pl.pallas_call(functools.partial(kernel, n, n_serve), out_shape=pltpu.VME...  74.9 us

profile of v4, /device:TPU:18, one launch (start us, length us, event | category | flops | bytes accessed | tf_op | source)
XLA Modules:
  0.0 75.9 jit_solution(12133160970980017977)
XLA Ops:
  0.0 74.9 %shard_map.73 = bf16[512,1024]{1,0:T(8,128)(2,1)S(1)} custom-call(s32[8]{0:T(128)} %seg_adapter.1, s32[8]{0:T(128)} %owner_map.1, s32[2]{0:T(128)} %seg_blocks.1, bf16[512,2048]{1,0:T(8,128)(2,1)} %tok_hbm.1, bf16[2048,4096]{1,0:T(8,128)(2,1)} %w_hbm.1, bf16[2,64,2048]{2,1,0:T(8,128)(2,1)} %down_hbm.1, bf16[2,64,1024]{2,1,0:T(8,128)(2,1)} %up_hbm.1), custom_call_target="tpu_custom_call" | custom-call | flops 8589934592 | bytes 19922944 | tf_op jit(solution)/shard_map/pallas_call | solution.py:450
  74.9 1.0 %copy.9 = bf16[512,1024]{1,0:T(8,128)(2,1)} copy(bf16[512,1024]{1,0:T(8,128)(2,1)S(1)} %shard_map.73) | data formatting | bytes 2097152
